TPU v7x, 32 devices: a whole 2x2x4 slice. The times are simulated.
32 devices in a mesh: groups: 2 (over y), space: 8 (over z, x), heads: 2 (over core).
Axes of the slice: x: 2, y: 2, z: 4, core: 2. Of those that a mesh axis runs over, the one named last changes fastest.
Arguments:
- queries: bfloat16 [2400, 1536], P(('groups', 'space'), 'heads'), parts along dimension 0, may hold values from -16 to 16
- latent_keys: bfloat16 [2400, 1536], P(('groups', 'space'), 'heads'), parts along dimension 0, may hold values from -9 to 9
- latent_values: bfloat16 [2400, 1536], P(('groups', 'space'), 'heads'), parts along dimension 0, may hold values from -6 to 6
- prompt: bfloat16 [512, 3072], P('groups'), parts along dimension 0, may hold values from -44 to 44
- key_weight: bfloat16 [3072, 1536], P('space', 'heads'), may hold values from -0.15625 to 0.15625
- value_weight: bfloat16 [3072, 1536], P('space', 'heads'), may hold values from -0.15625 to 0.15625
- out_weight: bfloat16 [1536, 3072], P('heads', 'space'), may hold values from -0.21875 to 0.21875
- tile_owner: int32 [16], P('groups'), parts along dimension 0, may hold values from 0 to 7, as said below
Outputs:
- block_output: bfloat16 [2400, 3072], P(('groups', 'space'), 'heads'), parts along dimension 0
There are 2 independent parts, one for each index of `groups`. A program takes and returns all parts, laid end to end along the dimension named above; an argument that names none is the same for every part. Nothing has to cross between parts.
Inputs may be any that keep to these rules, and one draw needn't show every extreme that they name: `tile_owner`: tile t = i * 2 + j of the 4 x 2 grid is held by slot a * 2 + b, with a = (i + r) mod 4 or a = (3 - i + r) mod 4 for one r, and b = j or b = 1 - j; r and each of the two alternatives are the same for all tiles.
All inputs are finite; a program needn't handle non-finite values.
Results may differ from a plain program's by a relative error of at most 0.0081.
Values may be sent and summed in bfloat16 or wider, within the bound.
A program may use at most 64 MiB of HBM per device.

v0:
```python
import jax
import jax.numpy as jnp
from jax import lax
from jax.sharding import PartitionSpec as P

HD = 128
RT = 16
RH = 56
TILE = 5
rope_theta = 256.0
eps_norm = 1e-06
masked_score = -1e30


def shifted(value, axis, steps):
    count = lax.axis_size(axis)
    pairs = [(source, (source + steps) % count) for source in range(count)]
    return lax.ppermute(value, axis, pairs)


def rope_tables(frame_pos, height_pos, width_pos):
    pairs_time = jnp.arange(RT // 2, dtype=jnp.float32)
    pairs_space = jnp.arange(RH // 2, dtype=jnp.float32)
    freq_time = rope_theta ** (-2.0 * pairs_time / RT)
    freq_space = rope_theta ** (-2.0 * pairs_space / RH)
    angles = jnp.concatenate(
        [
            frame_pos[:, None] * freq_time[None, :],
            height_pos[:, None] * freq_space[None, :],
            width_pos[:, None] * freq_space[None, :],
        ],
        axis=1,
    )
    return (jnp.cos(angles), jnp.sin(angles))


def rotate(stacked, cosine, sine_table):
    row_count = stacked.shape[0]
    head_total = stacked.shape[1]
    paired = stacked.reshape(row_count, head_total, HD // 2, 2)
    even_part = paired[..., 0]
    odd_part = paired[..., 1]
    cos_rows = cosine[:, None, :]
    sin_rows = sine_table[:, None, :]
    turned = jnp.stack(
        [even_part * cos_rows - odd_part * sin_rows, even_part * sin_rows + odd_part * cos_rows],
        axis=-1,
    )
    return turned.reshape(row_count, head_total * HD)


def normalize_keys(summed, head_total):
    row_count = summed.shape[0]
    half_width = summed.shape[1] // 2
    key_part = summed[:, :half_width].reshape(row_count, head_total, HD)
    key_part = key_part * lax.rsqrt(
        jnp.mean(key_part * key_part, axis=-1, keepdims=True) + eps_norm
    )
    return jnp.concatenate(
        [key_part.reshape(row_count, half_width), summed[:, half_width:]], axis=1
    ).astype(jnp.bfloat16)


def body(
    queries, latent_keys, latent_values, prompt, key_weight, value_weight, out_weight, tile_owner
):
    spaces = lax.axis_size("space")
    device = lax.axis_index("space")
    grid_h = min(8, spaces // 2)
    grid_w = spaces // grid_h
    tok_rows = queries.shape[0]
    head_width = queries.shape[1]
    head_count = head_width // HD
    tile_total = tile_owner.shape[0]
    tile_index = jnp.arange(tile_total, dtype=jnp.int32)
    own_tile = jnp.sum(jnp.where(tile_owner == device, tile_index, 0))
    tile_row = own_tile // grid_w
    tile_col = own_tile % grid_w
    anchor_slot = tile_owner[0]
    right_slot = tile_owner[min(1, tile_total - 1)]
    lower_slot = tile_owner[min(grid_w, tile_total - 1)]
    col_sign = jnp.where(right_slot % grid_w - anchor_slot % grid_w == -1, -1, 1)
    row_sign = jnp.where((lower_slot // grid_w - anchor_slot // grid_w) % grid_h == 1, 1, -1)
    cell_index = jnp.arange(tok_rows, dtype=jnp.int32)
    frame_pos = (cell_index // (TILE * TILE)).astype(jnp.float32)
    height_pos = (tile_row * TILE + cell_index // TILE % TILE).astype(jnp.float32)
    width_pos = (tile_col * TILE + cell_index % TILE).astype(jnp.float32)
    cosine, sine_table = rope_tables(frame_pos, height_pos, width_pos)
    query_rot = rotate(
        queries.astype(jnp.float32).reshape(tok_rows, head_count, HD), cosine, sine_table
    ).astype(jnp.bfloat16)
    key_rot = rotate(
        latent_keys.astype(jnp.float32).reshape(tok_rows, head_count, HD), cosine, sine_table
    ).astype(jnp.bfloat16)
    width_rows = key_weight.shape[0]
    text_cols = lax.dynamic_slice_in_dim(prompt, device * width_rows, width_rows, 1)
    both_weights = jnp.concatenate([key_weight, value_weight], axis=1)
    partial_text = jnp.dot(text_cols, both_weights, preferred_element_type=jnp.float32)
    summed_text = lax.psum(partial_text, "space")
    text_kv = normalize_keys(summed_text, head_count)
    kv_own = jnp.concatenate([key_rot, latent_values], axis=1)
    blocks = []
    valid_parts = []
    for row_step in (-1, 0, 1):
        for col_step in (-1, 0, 1):
            if row_step == 0 and col_step == 0:
                fetched = kv_own
            else:
                fetched = shifted(kv_own, "space", -(row_step * grid_w + col_step))
            near_row = tile_row + row_sign * row_step
            near_col = tile_col + col_sign * col_step
            inside = (near_row >= 0) & (near_row < grid_h) & (near_col >= 0) & (near_col < grid_w)
            blocks.append(fetched)
            valid_parts.append(jnp.zeros((tok_rows,), jnp.int32) + inside.astype(jnp.int32))
    blocks.append(text_kv)
    valid_parts.append(jnp.ones((text_kv.shape[0],), jnp.int32))
    keys_all = jnp.concatenate(blocks, axis=0)
    key_valid = jnp.concatenate(valid_parts, axis=0)
    score_scale = HD ** (-0.5)
    head_outputs = []
    for head_index in range(head_count):
        head_start = head_index * HD
        query_slice = query_rot[:, head_start : head_start + HD]
        key_slice = keys_all[:, head_start : head_start + HD]
        value_slice = keys_all[:, head_width + head_start : head_width + head_start + HD]
        scores = (
            lax.dot_general(
                query_slice, key_slice, (((1,), (1,)), ((), ())), preferred_element_type=jnp.float32
            )
            * score_scale
        )
        scores = jnp.where(key_valid[None, :] > 0, scores, masked_score)
        top_score = jnp.max(scores, axis=-1, keepdims=True)
        exponent = jnp.exp(scores - top_score)
        weights = (exponent / jnp.sum(exponent, axis=-1, keepdims=True)).astype(jnp.bfloat16)
        head_outputs.append(
            jnp.dot(weights, value_slice, preferred_element_type=jnp.float32).astype(jnp.bfloat16)
        )
    attended = jnp.concatenate(head_outputs, axis=1)
    partial_out = jnp.dot(
        attended,
        lax.all_gather(out_weight, "space", axis=1, tiled=True),
        preferred_element_type=jnp.float32,
    )
    summed_out = lax.psum_scatter(
        partial_out.astype(jnp.bfloat16), "heads", scatter_dimension=1, tiled=True
    )
    return summed_out


def solution(mesh):
    in_specs = (
        P(("groups", "space"), "heads"),
        P(("groups", "space"), "heads"),
        P(("groups", "space"), "heads"),
        P("groups", None),
        P("space", "heads"),
        P("space", "heads"),
        P("heads", "space"),
        P("groups"),
    )
    out_specs = P(("groups", "space"), "heads")
    return jax.shard_map(body, mesh=mesh, in_specs=in_specs, out_specs=out_specs, check_vma=False)
```

profile of v0, /device:TPU:0, one launch (start us, length us, event | category | flops | bytes accessed | tf_op | source)
XLA Modules:
  0.0 252.2 jit_solution(18399292161967376809)
XLA Ops:
  6.6 1.4 copy-done
  7.9 3.0 %fusion.6 = f32[256,1536]{1,0:T(8,128)} fusion(bf16[384,768]{1,0:T(8,128)(2,1)} %param.13, bf16[384,768]{1,0:T(8,128)(2,1)} %param.12, bf16[256,3072]{1,0:T(8,128)(2,1)S(1)} %copy-done, s32[]{:T(128)S(6)} %select_n.110), kind=kOutput, calls=%fused_computation.13 | convolution fusion | flops 304349184 | bytes 2949124 | tf_op jit(solution)/shard_map/dot_general | solution.py:98
  10.9 0.0 all-reduce.2.cloned.1.call-update
  10.9 0.0 all-gather.2.cloned.1.call-start
  11.0 0.7 all-gather.2.cloned.1.call-update
  11.7 0.0 reduce-scatter.2.cloned.1.call-start
  11.7 0.6 fusion.51
  15.0 0.2 copy.9
  15.2 0.5 reshape.201
  15.7 2.0 copy.10
  17.7 1.6 reshape.202
  19.3 0.1 broadcast_multiply_fusion.2
  19.4 0.1 broadcast_multiply_fusion.1
  19.5 0.2 fusion.42
  19.7 2.7 %subtract_convert_fusion.1 = (bf16[150,6,64,1]{0,3,2,1:T(2,128)(2,1)S(1)}, bf16[150,6,64,1]{0,3,2,1:T(2,128)(2,1)}, bf16[150,6,64,1]{0,3,2,1:T(2,128)(2,1)S(1)}, bf16[150,6,64,1]{0,3,2,1:T(2,128)(2,1)S(1)}) fusion(f32[150,6,64,2]{0,3,2,1:T(2,128)S(1)} %reshape.201, f32[150,64]{0,1:T(8,128)S(1)} %get-tuple-element.12, f32[150,64]{0,1:T(8,128)S(1)} %get-tuple-element.11, ...), kind=kLoop, calls=%fused_computation.69 | loop fusion | flops 921600 | bytes 1459200 | tf_op jit(solution)/shard_map/convert.7
  22.5 1.0 pad_maximum_fusion.3
  23.4 0.4 convert_element_type.111
  23.8 0.1 copy.11
  24.0 1.7 pad_maximum_fusion.1
  25.7 4.0 %collective-permute-start = (bf16[150,1536]{1,0:T(8,128)(2,1)}, bf16[150,1536]{1,0:T(8,128)(2,1)}, u32[]{:S(2)}, u32[]{:S(2)}) collective-permute-start(bf16[150,1536]{1,0:T(8,128)(2,1)} %pad_maximum_fusion.1), channel_id=1, source_target_pairs={{0,6},{2,8},{4,10},{6,12},{8,14},{10,0},{12,2},{14,4},{1,7},{3,9},... | collective-permute-start | bytes 1382408 | tf_op jit(solution)/shard_map/ppermute | solution.py:18
  29.7 1.6 collective-permute-start.1
  31.3 1.5 collective-permute-start.2
  32.8 3.2 %collective-permute-start.3 = (bf16[150,1536]{1,0:T(8,128)(2,1)}, bf16[150,1536]{1,0:T(8,128)(2,1)}, u32[]{:S(2)}, u32[]{:S(2)}) collective-permute-start(bf16[150,1536]{1,0:T(8,128)(2,1)} %pad_maximum_fusion.1), channel_id=1, source_target_pairs={{0,14},{2,0},{4,2},{6,4},{8,6},{10,8},{12,10},{14,12},{1,15},{3,1}... | collective-permute-start | bytes 1382408 | tf_op jit(solution)/shard_map/ppermute | solution.py:18
  36.0 0.5 collective-permute-start.4
  36.5 0.6 fusion.54
  43.3 2.0 pad_maximum_fusion.2
  45.3 1.1 convert_element_type.110
  46.5 0.1 concatenate.34
  46.6 91.5 %all-reduce.2.cloned.1.call-done = f32[256,1536]{1,0:T(8,128)} async-done(((f32[256,1536]{1,0:T(8,128)}), f32[256,1536]{1,0:T(8,128)}) %all-reduce.2.cloned.1.call-update) | async-done | bytes 1572880 | tf_op jit(solution)/shard_map/psum | solution.py:99
  138.1 1.2 slice_multiply_fusion
  139.3 0.3 copy.12
  139.6 0.1 reduce_sum.73
  139.6 0.1 mul.191
  139.7 0.3 copy.13
  140.0 1.2 slice.180
  141.1 0.0 collective-permute-done
  141.2 3.0 %collective-permute-start.5 = (bf16[150,1536]{1,0:T(8,128)(2,1)}, bf16[150,1536]{1,0:T(8,128)(2,1)S(1)}, u32[]{:S(2)}, u32[]{:S(2)}) collective-permute-start(bf16[150,1536]{1,0:T(8,128)(2,1)} %pad_maximum_fusion.1), channel_id=1, source_target_pairs={{0,10},{2,12},{4,14},{6,0},{8,2},{10,4},{12,6},{14,8},{1,11},{3,13... | collective-permute-start | bytes 1382408 | tf_op jit(solution)/shard_map/ppermute | solution.py:18
  144.1 1.2 multiply_convert_fusion
  145.3 0.1 pad_maximum_fusion
  145.4 0.0 collective-permute-done.1
  145.4 16.0 %collective-permute-done.5 = bf16[150,1536]{1,0:T(8,128)(2,1)S(1)} collective-permute-done((bf16[150,1536]{1,0:T(8,128)(2,1)}, bf16[150,1536]{1,0:T(8,128)(2,1)S(1)}, u32[]{:S(2)}, u32[]{:S(2)}) %collective-permute-start.5) | collective-permute-done | bytes 460832 | tf_op jit(solution)/shard_map/ppermute | solution.py:18
  161.5 34.4 %concatenate.39 = bf16[1606,1536]{1,0:T(8,128)(2,1)} concatenate(bf16[150,1536]{1,0:T(8,128)(2,1)} %collective-permute-done, bf16[150,1536]{1,0:T(8,128)(2,1)} %collective-permute-done.1, bf16[150,1536]{1,0:T(8,128)(2,1)} %collective-permute-done.2, bf16[150,1536]{1,0:T(8,128)(2,1)} %collective-permute-done.2, bf16[150,1536]{1,0:T(8,128)(2,1)} %pad_maximum_fusion.1, ...), dimensions={0} | concatenate | bytes 9867264 | tf_op jit(solution)/shard_map/concatenate | solution.py:117
  195.9 1.6 fusion.55
  197.5 0.3 fusion.16
  197.8 1.6 fusion.56
  199.4 0.3 fusion.17
  199.7 1.7 fusion.57
  201.4 0.3 fusion.18
  201.7 1.6 fusion.58
  203.3 0.3 fusion.19
  203.5 1.6 fusion.59
  205.1 0.3 fusion.20
  205.4 1.6 fusion.60
  207.0 0.3 fusion.21
  207.3 0.4 fusion.15
  207.7 0.4 fusion.14
  208.2 0.4 fusion.13
  208.6 0.4 fusion.12
  209.0 0.4 fusion.11
  209.4 0.4 fusion.10
  209.9 22.8 %all-gather.2.cloned.1.call-done = bf16[768,3072]{1,0:T(8,128)(2,1)} async-done(((bf16[768,384]{1,0:T(8,128)(2,1)}), bf16[768,3072]{1,0:T(8,128)(2,1)}) %all-gather.2.cloned.1.call-update) | async-done | bytes 4718608 | tf_op jit(solution)/shard_map/all_gather | solution.py:142
  232.6 4.2 %convolution_convert_fusion = bf16[150,3072]{1,0:T(8,128)(2,1)} fusion(bf16[150,768]{1,0:T(8,128)(2,1)S(1)} %fusion.10, bf16[768,3072]{1,0:T(8,128)(2,1)} %all-gather.2.cloned.1.call-done), kind=kOutput, calls=%fused_computation | convolution fusion | flops 708249600 | bytes 5870592 | tf_op jit(solution)/shard_map/dot_general | solution.py:140
  236.8 0.0 reduce-scatter.2.cloned.1.call-update
  236.8 8.8 %reduce-scatter.2.cloned.1.call-done = bf16[150,1536]{1,0:T(8,128)(2,1)} async-done(((bf16[150,3072]{1,0:T(8,128)(2,1)}), bf16[150,1536]{1,0:T(8,128)(2,1)}) %reduce-scatter.2.cloned.1.call-update) | async-done | bytes 460816 | tf_op jit(solution)/shard_map/reduce_scatter | solution.py:145
  (27 shorter events, 0.1 us)
Async XLA Ops:
  6.5 1.4 copy-start
  6.5 5.2 %copy-start.3 = (s32[8]{0:T(128)S(1)}, s32[8]{0:T(128)}, u32[]{:S(2)}) copy-start(s32[8]{0:T(128)} %param.15) | copy-start | bytes 100
  6.5 8.4 %copy-start.2 = (bf16[150,768]{1,0:T(8,128)(2,1)S(1)}, bf16[150,768]{1,0:T(8,128)(2,1)}, u32[]{:S(2)}) copy-start(bf16[150,768]{1,0:T(8,128)(2,1)} %param.8) | copy-start | bytes 691204
  6.5 131.5 %all-reduce.2.cloned.1.call-start = ((), (), s32[]{:S(2)}) async-start(), calls=%async_computation.1 | async-start | bytes 3145728 | tf_op jit(solution)/shard_map/psum | solution.py:99
  10.9 221.7 %all-gather.2.cloned.1.call-start = ((), (), s32[]{:S(2)}) async-start(), calls=%async_computation.2 | async-start | bytes 5308416 | tf_op jit(solution)/shard_map/all_gather | solution.py:142
  11.7 234.0 %reduce-scatter.2.cloned.1.call-start = ((), (), s32[]{:S(2)}) async-start(), calls=%async_computation.3 | async-start | bytes 1400832 | tf_op jit(solution)/shard_map/reduce_scatter | solution.py:145
  25.7 115.4 %collective-permute-start = (bf16[150,1536]{1,0:T(8,128)(2,1)}, bf16[150,1536]{1,0:T(8,128)(2,1)}, u32[]{:S(2)}, u32[]{:S(2)}) collective-permute-start(bf16[150,1536]{1,0:T(8,128)(2,1)} %pad_maximum_fusion.1), channel_id=1, source_target_pairs={{0,6},{2,8},{4,10},{6,12},{8,14},{10,0},{12,2},{14,4},{1,7},{3,9},... | collective-permute-start | bytes 1382408 | tf_op jit(solution)/shard_map/ppermute | solution.py:18
  29.7 115.7 %collective-permute-start.1 = (bf16[150,1536]{1,0:T(8,128)(2,1)}, bf16[150,1536]{1,0:T(8,128)(2,1)}, u32[]{:S(2)}, u32[]{:S(2)}) collective-permute-start(bf16[150,1536]{1,0:T(8,128)(2,1)} %pad_maximum_fusion.1), channel_id=1, source_target_pairs={{0,4},{2,6},{4,8},{6,10},{8,12},{10,14},{12,0},{14,2},{1,5},{3,7},... | collective-permute-start | bytes 1382408 | tf_op jit(solution)/shard_map/ppermute | solution.py:18
  31.3 114.1 %collective-permute-start.2 = (bf16[150,1536]{1,0:T(8,128)(2,1)}, bf16[150,1536]{1,0:T(8,128)(2,1)}, u32[]{:S(2)}, u32[]{:S(2)}) collective-permute-start(bf16[150,1536]{1,0:T(8,128)(2,1)} %pad_maximum_fusion.1), channel_id=1, source_target_pairs={{0,2},{2,4},{4,6},{6,8},{8,10},{10,12},{12,14},{14,0},{1,3},{3,5},... | collective-permute-start | bytes 1382408 | tf_op jit(solution)/shard_map/ppermute | solution.py:18
  32.8 112.6 %collective-permute-start.3 = (bf16[150,1536]{1,0:T(8,128)(2,1)}, bf16[150,1536]{1,0:T(8,128)(2,1)}, u32[]{:S(2)}, u32[]{:S(2)}) collective-permute-start(bf16[150,1536]{1,0:T(8,128)(2,1)} %pad_maximum_fusion.1), channel_id=1, source_target_pairs={{0,14},{2,0},{4,2},{6,4},{8,6},{10,8},{12,10},{14,12},{1,15},{3,1}... | collective-permute-start | bytes 1382408 | tf_op jit(solution)/shard_map/ppermute | solution.py:18
  36.0 109.4 %collective-permute-start.4 = (bf16[150,1536]{1,0:T(8,128)(2,1)}, bf16[150,1536]{1,0:T(8,128)(2,1)}, u32[]{:S(2)}, u32[]{:S(2)}) collective-permute-start(bf16[150,1536]{1,0:T(8,128)(2,1)} %pad_maximum_fusion.1), channel_id=1, source_target_pairs={{0,12},{2,14},{4,0},{6,2},{8,4},{10,6},{12,8},{14,10},{1,13},{3,15... | collective-permute-start | bytes 1382408 | tf_op jit(solution)/shard_map/ppermute | solution.py:18
  141.2 20.3 %collective-permute-start.5 = (bf16[150,1536]{1,0:T(8,128)(2,1)}, bf16[150,1536]{1,0:T(8,128)(2,1)S(1)}, u32[]{:S(2)}, u32[]{:S(2)}) collective-permute-start(bf16[150,1536]{1,0:T(8,128)(2,1)} %pad_maximum_fusion.1), channel_id=1, source_target_pairs={{0,10},{2,12},{4,14},{6,0},{8,2},{10,4},{12,6},{14,8},{1,11},{3,13... | collective-permute-start | bytes 1382408 | tf_op jit(solution)/shard_map/ppermute | solution.py:18
  199.6 7.7 %copy-start.1 = (bf16[1606,1536]{1,0:T(8,128)(2,1)S(1)}, bf16[1606,1536]{1,0:T(8,128)(2,1)}, u32[]{:S(2)}) copy-start(bf16[1606,1536]{1,0:T(8,128)(2,1)} %concatenate.39) | copy-start | bytes 14800900
Sparse Core Ops, SparseCore 0:
  11.1 126.9 all-reduce.1
  140.1 92.4 all-gather.1
  237.0 8.6 reduce-scatter.1
where the time goes:
time: 254 us; the launch traced here: 252 us
  waiting for transfers between devices  140 us (55%)
  local copies, waits for them, and re-layouts  44.1 us (17%)
  between operations  22.3 us (9%)
  matrix products  19.3 us (8%)
  starting transfers between devices  13.8 us (5%)
  other arithmetic  12.8 us (5%)
    psum x1, waiting for transfers between devices, body(): summed_text = lax.psum(partial_text, 'space')  91.5 us
    concatenate x1, local copies, waits for them, and re-layouts, body(): keys_all = jnp.concatenate(blocks, axis=0)  34.4 us
    all_gather x1, waiting for transfers between devices, body(): lax.all_gather(out_weight, 'space', axis=1, tiled=True)  22.8 us
    ppermute x6, waiting for transfers between devices, shifted(): return lax.ppermute(value, axis, pairs)  16.1 us
    ppermute x6, starting transfers between devices, shifted(): return lax.ppermute(value, axis, pairs)  13.7 us
    dot_general x6, matrix products, body(): lax.dot_general(query_slice, key_slice, (((1,), (1,)), ((), ())), preferr...  9.63 us
    reduce_scatter x1, waiting for transfers between devices, body(): lax.psum_scatter(partial_out.astype(jnp.bfloat16), 'heads', scatter_dimen...  8.8 us
  transfers between devices with their start and end apart: 9, of which 4 were waited for; matrix products, arithmetic and copies ran while one was open for 27% of the time, Pallas kernels for 0%

commit v1 on v0

--- a/solution.py
+++ b/solution.py
@@ -96,7 +96,11 @@
     text_cols = lax.dynamic_slice_in_dim(prompt, device * width_rows, width_rows, 1)
     both_weights = jnp.concatenate([key_weight, value_weight], axis=1)
     partial_text = jnp.dot(text_cols, both_weights, preferred_element_type=jnp.float32)
-    summed_text = lax.psum(partial_text, "space")
+    summed_text = partial_text
+    for hop in (1, 2, 4):
+        summed_text = summed_text + lax.ppermute(
+            summed_text, "space", [(dev, dev ^ hop) for dev in range(8)]
+        )
     text_kv = normalize_keys(summed_text, head_count)
     kv_own = jnp.concatenate([key_rot, latent_values], axis=1)
     blocks = []

time: 254 us -> 346 us (1.36)
  waiting for transfers between devices: 140 us -> 208 us
  local copies, waits for them, and re-layouts: 44.1 us -> 58 us
  other arithmetic: 12.8 us -> 22.2 us
    ppermute x0 -> x3, waiting for transfers between devices: none -> 170 us  [body(): lax.ppermute(summed_text, 'space', [(dev, dev ^ hop) for dev in range(8)])]
    psum x1 -> x0, waiting for transfers between devices: 91.5 us -> none  [body(): summed_text = lax.psum(partial_text, 'space')]
    all_gather x1, waiting for transfers between devices: 22.8 us -> 0.02 us  [body(): lax.all_gather(out_weight, 'space', axis=1, tiled=True)]
    ppermute x6, waiting for transfers between devices: 16.1 us -> 28.7 us  [shifted(): return lax.ppermute(value, axis, pairs)]
    ppermute x0 -> x3, starting transfers between devices: none -> 7.42 us  [body(): lax.ppermute(summed_text, 'space', [(dev, dev ^ hop) for dev in range(8)])]
    ppermute x6, starting transfers between devices: 13.7 us -> 7.24 us  [shifted(): return lax.ppermute(value, axis, pairs)]
    add x0 -> x3, other arithmetic: none -> 5.54 us  [body(): summed_text + lax.ppermute(summed_text, 'space', [(dev, dev ^ hop) for de...]
    another operation x4, local copies, waits for them, and re-layouts: 4.23 us -> 8.03 us  [rotate(): paired = stacked.reshape(row_count, head_total, HD // 2, 2)]
  transfers between devices with their start and end apart: 9 -> 11, of which waited for: 4 -> 6; matrix products, arithmetic and copies ran while one was open for 27% -> 26% of each run, Pallas kernels for 0% -> 0%
where the time goes in v1:
time: 346 us; the launch traced here: 344 us
  waiting for transfers between devices  208 us (60%)
  local copies, waits for them, and re-layouts  58 us (17%)
  between operations  23.2 us (7%)
  other arithmetic  22.2 us (6%)
  matrix products  18.1 us (5%)
  starting transfers between devices  14.7 us (4%)
    ppermute x3, waiting for transfers between devices, body(): lax.ppermute(summed_text, 'space', [(dev, dev ^ hop) for dev in range(8)])  170 us
    concatenate x1, local copies, waits for them, and re-layouts, body(): keys_all = jnp.concatenate(blocks, axis=0)  36.1 us
    ppermute x6, waiting for transfers between devices, shifted(): return lax.ppermute(value, axis, pairs)  28.7 us
    dot_general x6, matrix products, body(): lax.dot_general(query_slice, key_slice, (((1,), (1,)), ((), ())), preferr...  9.61 us
    reduce_scatter x1, waiting for transfers between devices, body(): lax.psum_scatter(partial_out.astype(jnp.bfloat16), 'heads', scatter_dimen...  9.42 us
    another operation x4, local copies, waits for them, and re-layouts, rotate(): paired = stacked.reshape(row_count, head_total, HD // 2, 2)  8.03 us
    ppermute x3, starting transfers between devices, body(): lax.ppermute(summed_text, 'space', [(dev, dev ^ hop) for dev in range(8)])  7.42 us
    ppermute x6, starting transfers between devices, shifted(): return lax.ppermute(value, axis, pairs)  7.24 us
  transfers between devices with their start and end apart: 11, of which 6 were waited for; matrix products, arithmetic and copies ran while one was open for 26% of the time, Pallas kernels for 0%

profile of v1, /device:TPU:0, one launch (start us, length us, event | category | flops | bytes accessed | tf_op | source)
XLA Modules:
  0.0 344.0 jit_solution(192976522015262973)
XLA Ops:
  6.5 1.4 copy-done
  7.9 1.8 fusion.6
  9.8 3.0 collective-permute-start.6
  12.8 34.4 %collective-permute-done.6 = f32[256,1536]{1,0:T(8,128)S(1)} collective-permute-done((f32[256,1536]{1,0:T(8,128)S(1)}, f32[256,1536]{1,0:T(8,128)S(1)}, u32[]{:S(2)}, u32[]{:S(2)}) %collective-permute-start.6) | collective-permute-done | bytes 1572896 | tf_op jit(solution)/shard_map/ppermute | solution.py:101
  47.2 1.4 add.170
  48.6 1.8 collective-permute-start.7
  50.4 0.0 all-gather.2.cloned.1.call-update
  50.4 0.0 reduce-scatter.2.cloned.1.call-start
  50.5 0.6 fusion.51
  53.8 0.1 broadcast_multiply_fusion.1
  53.9 49.6 %collective-permute-done.7 = f32[256,1536]{1,0:T(8,128)} collective-permute-done((f32[256,1536]{1,0:T(8,128)}, f32[256,1536]{1,0:T(8,128)}, u32[]{:S(2)}, u32[]{:S(2)}) %collective-permute-start.7) | collective-permute-done | bytes 1572896 | tf_op jit(solution)/shard_map/ppermute | solution.py:101
  103.4 2.1 add.171
  105.5 2.6 collective-permute-start.8
  108.1 0.1 broadcast_multiply_fusion.2
  108.2 1.1 copy.9
  109.2 2.5 reshape.201
  111.7 2.0 copy.10
  113.7 2.5 reshape.202
  116.2 0.2 fusion.42
  116.4 4.1 %subtract_convert_fusion.1 = (bf16[150,6,64,1]{0,3,2,1:T(2,128)(2,1)S(1)}, bf16[150,6,64,1]{0,3,2,1:T(2,128)(2,1)}, bf16[150,6,64,1]{0,3,2,1:T(2,128)(2,1)S(1)}, bf16[150,6,64,1]{0,3,2,1:T(2,128)(2,1)S(1)}) fusion(f32[150,6,64,2]{0,3,2,1:T(2,128)} %reshape.201, f32[150,64]{0,1:T(8,128)S(1)} %get-tuple-element.12, f32[150,64]{0,1:T(8,128)S(1)} %get-tuple-element.11, ...), kind=kLoop, calls=%fused_computation.69 | loop fusion | flops 921600 | bytes 1459200 | tf_op jit(solution)/shard_map/convert.7
  120.6 1.7 pad_maximum_fusion.3
  122.3 2.1 convert_element_type.111
  124.4 1.8 copy.11
  126.2 1.9 pad_maximum_fusion.1
  128.1 2.5 collective-permute-start
  130.6 0.9 collective-permute-start.2
  131.5 3.8 %collective-permute-start.3 = (bf16[150,1536]{1,0:T(8,128)(2,1)}, bf16[150,1536]{1,0:T(8,128)(2,1)}, u32[]{:S(2)}, u32[]{:S(2)}) collective-permute-start(bf16[150,1536]{1,0:T(8,128)(2,1)} %pad_maximum_fusion.1), channel_id=1, source_target_pairs={{0,14},{2,0},{4,2},{6,4},{8,6},{10,8},{12,10},{14,12},{1,15},{3,1}... | collective-permute-start | bytes 1382408 | tf_op jit(solution)/shard_map/ppermute | solution.py:18
  135.3 0.7 fusion.54
  143.0 2.7 pad_maximum_fusion.2
  145.7 2.1 convert_element_type.110
  147.9 0.1 concatenate.34
  148.0 85.6 %collective-permute-done.8 = f32[256,1536]{1,0:T(8,128)} collective-permute-done((f32[256,1536]{1,0:T(8,128)S(1)}, f32[256,1536]{1,0:T(8,128)}, u32[]{:S(2)}, u32[]{:S(2)}) %collective-permute-start.8) | collective-permute-done | bytes 1572896 | tf_op jit(solution)/shard_map/ppermute | solution.py:101
  233.6 2.1 add.172
  235.7 0.9 slice_multiply_fusion
  236.7 2.3 copy.12
  239.0 1.2 reduce_sum.73
  240.2 1.0 mul.191
  241.2 2.3 copy.13
  243.4 11.2 %collective-permute-done = bf16[150,1536]{1,0:T(8,128)(2,1)} collective-permute-done((bf16[150,1536]{1,0:T(8,128)(2,1)}, bf16[150,1536]{1,0:T(8,128)(2,1)}, u32[]{:S(2)}, u32[]{:S(2)}) %collective-permute-start) | collective-permute-done | bytes 460832 | tf_op jit(solution)/shard_map/ppermute | solution.py:18
  254.6 1.2 multiply_convert_fusion
  255.9 0.1 pad_maximum_fusion
  256.0 17.5 %collective-permute-done.5 = bf16[150,1536]{1,0:T(8,128)(2,1)} collective-permute-done((bf16[150,1536]{1,0:T(8,128)(2,1)}, bf16[150,1536]{1,0:T(8,128)(2,1)}, u32[]{:S(2)}, u32[]{:S(2)}) %collective-permute-start.5) | collective-permute-done | bytes 460832 | tf_op jit(solution)/shard_map/ppermute | solution.py:18
  273.4 36.1 %concatenate.39 = bf16[1606,1536]{1,0:T(8,128)(2,1)} concatenate(bf16[150,1536]{1,0:T(8,128)(2,1)} %collective-permute-done, bf16[150,1536]{1,0:T(8,128)(2,1)} %collective-permute-done.1, bf16[150,1536]{1,0:T(8,128)(2,1)} %collective-permute-done.2, bf16[150,1536]{1,0:T(8,128)(2,1)} %collective-permute-done.2, bf16[150,1536]{1,0:T(8,128)(2,1)} %pad_maximum_fusion.1, ...), dimensions={0} | concatenate | bytes 9867264 | tf_op jit(solution)/shard_map/concatenate | solution.py:121
  309.6 1.7 fusion.55
  311.3 0.3 fusion.16
  311.6 1.6 fusion.56
  313.1 0.3 fusion.17
  313.4 1.6 fusion.57
  315.0 0.3 fusion.18
  315.3 1.6 fusion.58
  316.9 0.3 fusion.19
  317.2 1.6 fusion.59
  318.8 0.3 fusion.20
  319.1 1.6 fusion.60
  320.7 0.3 fusion.21
  321.0 0.4 fusion.15
  321.4 0.4 fusion.14
  321.8 0.4 fusion.13
  322.2 0.4 fusion.12
  322.6 0.4 fusion.11
  323.1 0.4 fusion.10
  323.5 0.0 all-gather.2.cloned.1.call-done
  323.5 4.2 %convolution_convert_fusion = bf16[150,3072]{1,0:T(8,128)(2,1)} fusion(bf16[150,768]{1,0:T(8,128)(2,1)S(1)} %fusion.10, bf16[768,3072]{1,0:T(8,128)(2,1)} %all-gather.2.cloned.1.call-done), kind=kOutput, calls=%fused_computation | convolution fusion | flops 708249600 | bytes 5870592 | tf_op jit(solution)/shard_map/dot_general | solution.py:144
  327.7 9.4 %reduce-scatter.2.cloned.1.call-done = bf16[150,1536]{1,0:T(8,128)(2,1)} async-done(((bf16[150,3072]{1,0:T(8,128)(2,1)}), bf16[150,1536]{1,0:T(8,128)(2,1)}) %reduce-scatter.2.cloned.1.call-update) | async-done | bytes 460816 | tf_op jit(solution)/shard_map/reduce_scatter | solution.py:149
  (38 shorter events, 0.2 us)
Async XLA Ops:
  6.5 1.4 copy-start
  6.5 43.9 %copy-start.3 = (s32[8]{0:T(128)S(1)}, s32[8]{0:T(128)}, u32[]{:S(2)}) copy-start(s32[8]{0:T(128)} %param.15) | copy-start | bytes 100
  6.5 317.0 %all-gather.2.cloned.1.call-start = ((), (), s32[]{:S(2)}) async-start(), calls=%async_computation.1 | async-start | bytes 5308416 | tf_op jit(solution)/shard_map/all_gather | solution.py:146
  9.8 98.4 %copy-start.2 = (bf16[150,768]{1,0:T(8,128)(2,1)S(1)}, bf16[150,768]{1,0:T(8,128)(2,1)}, u32[]{:S(2)}) copy-start(bf16[150,768]{1,0:T(8,128)(2,1)} %param.8) | copy-start | bytes 691204
  9.8 37.4 %collective-permute-start.6 = (f32[256,1536]{1,0:T(8,128)S(1)}, f32[256,1536]{1,0:T(8,128)S(1)}, u32[]{:S(2)}, u32[]{:S(2)}) collective-permute-start(f32[256,1536]{1,0:T(8,128)S(1)} %fusion.6), channel_id=1, source_target_pairs={{0,2},{2,0},{4,6},{6,4},{8,10},{10,8},{12,14},{14,12},{1,3},{3,1},... | collective-permute-start | bytes 4718600 | tf_op jit(solution)/shard_map/ppermute | solution.py:101
  48.6 54.9 %collective-permute-start.7 = (f32[256,1536]{1,0:T(8,128)}, f32[256,1536]{1,0:T(8,128)}, u32[]{:S(2)}, u32[]{:S(2)}) collective-permute-start(f32[256,1536]{1,0:T(8,128)} %add.170), channel_id=1, source_target_pairs={{0,4},{2,6},{4,0},{6,2},{8,12},{10,14},{12,8},{14,10},{1,5},{3,7},... | collective-permute-start | bytes 4718600 | tf_op jit(solution)/shard_map/ppermute | solution.py:101
  50.4 286.7 %reduce-scatter.2.cloned.1.call-start = ((), (), s32[]{:S(2)}) async-start(), calls=%async_computation.2 | async-start | bytes 1400832 | tf_op jit(solution)/shard_map/reduce_scatter | solution.py:149
  105.5 16.8 %copy-start.1 = (f32[256,1536]{1,0:T(8,128)}, f32[256,1536]{1,0:T(8,128)S(1)}, u32[]{:S(2)}) copy-start(f32[256,1536]{1,0:T(8,128)S(1)} %add.171) | copy-start | bytes 4718596
  105.5 128.1 %collective-permute-start.8 = (f32[256,1536]{1,0:T(8,128)S(1)}, f32[256,1536]{1,0:T(8,128)}, u32[]{:S(2)}, u32[]{:S(2)}) collective-permute-start(f32[256,1536]{1,0:T(8,128)S(1)} %add.171), channel_id=1, source_target_pairs={{0,8},{2,10},{4,12},{6,14},{8,0},{10,2},{12,4},{14,6},{1,9},{3,11}... | collective-permute-start | bytes 4718600 | tf_op jit(solution)/shard_map/ppermute | solution.py:101
  128.1 126.6 %collective-permute-start = (bf16[150,1536]{1,0:T(8,128)(2,1)}, bf16[150,1536]{1,0:T(8,128)(2,1)}, u32[]{:S(2)}, u32[]{:S(2)}) collective-permute-start(bf16[150,1536]{1,0:T(8,128)(2,1)} %pad_maximum_fusion.1), channel_id=1, source_target_pairs={{0,6},{2,8},{4,10},{6,12},{8,14},{10,0},{12,2},{14,4},{1,7},{3,9},... | collective-permute-start | bytes 1382408 | tf_op jit(solution)/shard_map/ppermute | solution.py:18
  130.6 125.3 %collective-permute-start.1 = (bf16[150,1536]{1,0:T(8,128)(2,1)}, bf16[150,1536]{1,0:T(8,128)(2,1)}, u32[]{:S(2)}, u32[]{:S(2)}) collective-permute-start(bf16[150,1536]{1,0:T(8,128)(2,1)} %pad_maximum_fusion.1), channel_id=1, source_target_pairs={{0,4},{2,6},{4,8},{6,10},{8,12},{10,14},{12,0},{14,2},{1,5},{3,7},... | collective-permute-start | bytes 1382408 | tf_op jit(solution)/shard_map/ppermute | solution.py:18
  130.6 125.4 %collective-permute-start.2 = (bf16[150,1536]{1,0:T(8,128)(2,1)}, bf16[150,1536]{1,0:T(8,128)(2,1)}, u32[]{:S(2)}, u32[]{:S(2)}) collective-permute-start(bf16[150,1536]{1,0:T(8,128)(2,1)} %pad_maximum_fusion.1), channel_id=1, source_target_pairs={{0,2},{2,4},{4,6},{6,8},{8,10},{10,12},{12,14},{14,0},{1,3},{3,5},... | collective-permute-start | bytes 1382408 | tf_op jit(solution)/shard_map/ppermute | solution.py:18
  131.5 124.5 %collective-permute-start.3 = (bf16[150,1536]{1,0:T(8,128)(2,1)}, bf16[150,1536]{1,0:T(8,128)(2,1)}, u32[]{:S(2)}, u32[]{:S(2)}) collective-permute-start(bf16[150,1536]{1,0:T(8,128)(2,1)} %pad_maximum_fusion.1), channel_id=1, source_target_pairs={{0,14},{2,0},{4,2},{6,4},{8,6},{10,8},{12,10},{14,12},{1,15},{3,1}... | collective-permute-start | bytes 1382408 | tf_op jit(solution)/shard_map/ppermute | solution.py:18
  233.6 22.3 %collective-permute-start.4 = (bf16[150,1536]{1,0:T(8,128)(2,1)}, bf16[150,1536]{1,0:T(8,128)(2,1)}, u32[]{:S(2)}, u32[]{:S(2)}) collective-permute-start(bf16[150,1536]{1,0:T(8,128)(2,1)} %pad_maximum_fusion.1), channel_id=1, source_target_pairs={{0,12},{2,14},{4,0},{6,2},{8,4},{10,6},{12,8},{14,10},{1,13},{3,15... | collective-permute-start | bytes 1382408 | tf_op jit(solution)/shard_map/ppermute | solution.py:18
  254.6 18.8 %collective-permute-start.5 = (bf16[150,1536]{1,0:T(8,128)(2,1)}, bf16[150,1536]{1,0:T(8,128)(2,1)}, u32[]{:S(2)}, u32[]{:S(2)}) collective-permute-start(bf16[150,1536]{1,0:T(8,128)(2,1)} %pad_maximum_fusion.1), channel_id=1, source_target_pairs={{0,10},{2,12},{4,14},{6,0},{8,2},{10,4},{12,6},{14,8},{1,11},{3,13... | collective-permute-start | bytes 1382408 | tf_op jit(solution)/shard_map/ppermute | solution.py:18
  309.6 11.4 %slice-start = ((s8[4939776]{0:T(1024)(128)(4,1)}), s8[4194304]{0:T(1024)(128)(4,1)S(1)}, s32[]{:S(2)}) async-start(s8[4939776]{0:T(1024)(128)(4,1)} %bitcast.15), calls=%async_computation.3 | async-start | bytes 8388608
  315.0 5.9 %slice-start.1 = ((s8[4939776]{0:T(1024)(128)(4,1)}), s8[745472]{0:T(1024)(128)(4,1)S(1)}, s32[]{:S(2)}) async-start(s8[4939776]{0:T(1024)(128)(4,1)} %bitcast.15), calls=%async_computation.4 | async-start | bytes 1490944
Sparse Core Ops, SparseCore 0:
  50.5 168.4 all-gather.1
  327.9 9.2 reduce-scatter.1
